TPU v7x, 32 devices: a whole 2x2x4 slice. The times are simulated.
32 devices in a mesh: parts: 2 (over x), row: 16 (over z, y, core).
Axes of the slice: x: 2, y: 2, z: 4, core: 2. Of those that a mesh axis runs over, the one named last changes fastest.
Arguments:
- density: bfloat16 [39936, 936], P(('parts', 'row')), parts along dimension 0, may hold values from -0.59765625 to 0.59765625
- tile_mask: int32 [384, 9], P('parts'), parts along dimension 0, may hold values from 0 to 1, as said below
- padding: int32 [384], P('parts'), parts along dimension 0, may hold values from 0 to 26
Outputs:
- purified: bfloat16 [39936, 936], P(('parts', 'row')), parts along dimension 0
There are 2 independent parts, one for each index of `parts`. A program takes and returns all parts, laid end to end along the dimension named above; each array names one. Nothing has to cross between parts.
Inputs may be any that keep to these rules, and one draw needn't show every extreme that they name: `tile_mask`: centre column 4 is 1 in every row; entries whose tile column i + c - 4 falls outside 0 to 191 are 0.
All inputs are finite; a program needn't handle non-finite values.
Results may differ from a plain program's by a relative error of at most 0.006.
Values may be sent and summed in bfloat16 or wider, within the bound.
A program may use at most 128 MiB of HBM per device.

v0:
```python
import functools

import jax
import jax.numpy as jnp
from jax import lax
from jax.experimental import pallas as pl
from jax.experimental.pallas import tpu as pltpu
from jax.sharding import PartitionSpec as P

B = 104
H = 4
BAND = 9
PR = 2 * B
PW = 256
NP = 5
WIDE = NP * PW
FAR = 4
OWN = 6
ALL = OWN + 2 * FAR
MESH = pl.DeviceIdType.MESH


def kernel(count, tiles, density, tile_mask, padding, out, x, f, s, t32, cm,
           send_sem, recv_sem, own_sem):
    me = lax.axis_index("row")
    odd = lax.rem(me, 2)
    even = odd == 0
    has_up = me > 0
    has_down = me < count - 1
    first = me * (2 * OWN) - 2 * FAR

    own = pltpu.make_async_copy(density, x.at[pl.ds(FAR * PR, OWN * PR), :], own_sem)
    own.start()

    barrier = pltpu.get_barrier_semaphore()

    @pl.when(has_up)
    def _():
        pl.semaphore_signal(barrier, inc=1, device_id={"row": me - 1}, device_id_type=MESH)

    @pl.when(has_down)
    def _():
        pl.semaphore_signal(barrier, inc=1, device_id={"row": me + 1}, device_id_type=MESH)

    pl.semaphore_wait(barrier, has_up.astype(jnp.int32) + has_down.astype(jnp.int32))

    def piece(src_row, dst_row, rows, lane, width, slot, where):
        return pltpu.make_async_remote_copy(
            src_ref=density.at[pl.ds(src_row, rows), pl.ds(lane, width)],
            dst_ref=x.at[pl.ds(dst_row, rows), pl.ds(lane, width)],
            send_sem=send_sem.at[slot], recv_sem=recv_sem.at[slot],
            device_id={"row": where}, device_id_type=MESH)

    full = BAND * B

    def tail():
        return [piece(4 * PR, 2 * PR, 2 * PR, 0, full, 0, me + 1),
                piece(3 * PR, 1 * PR, PR, 512, full - 512, 1, me + 1),
                piece(2 * PR, 0, PR, 640, full - 640, 2, me + 1)]

    def head():
        return [piece(0, 10 * PR, 2 * PR, 0, full, 3, me - 1),
                piece(2 * PR, 12 * PR, PR, 0, 512, 4, me - 1),
                piece(3 * PR, 13 * PR, PR, 0, 256, 5, me - 1)]

    @pl.when(has_down)
    def _():
        for c in tail():
            c.start()

    @pl.when(has_up)
    def _():
        for c in head():
            c.start()

    lane = lax.broadcasted_iota(jnp.int32, (1, WIDE), 1)
    inner = lane % PW
    second = (inner >= B).astype(jnp.int32)
    slot_of = (lane // PW) * 2 + second
    z = inner - B * second

    def masks(p, carry):
        for a in range(2):
            t = first + 2 * p + a
            tc = jnp.clip(t, 0, tiles - 1)
            lim = jnp.zeros((1, WIDE), jnp.int32)
            for c in range(BAND):
                j = jnp.clip(t + c - H, 0, tiles - 1)
                lim = jnp.where(slot_of == a + c, tile_mask[tc, c] * (B - padding[j]), lim)
            cm[pl.ds(pl.multiple_of(p * 16 + a * 8, 8), 8), :] = jnp.broadcast_to(
                jnp.where((z < lim) & (z < B), 1.0, 0.0), (8, WIDE))
        return carry

    lax.fori_loop(0, ALL, masks, 0)
    t32[...] = jnp.zeros_like(t32)
    f[...] = jnp.zeros_like(f)

    def mask_row(p, a):
        return cm[pl.ds(pl.multiple_of(p * 16 + a * 8, 8), 1), :]

    def rows_of(p):
        return pl.ds(pl.multiple_of(p * PR, 16), PR)

    row = lax.broadcasted_iota(jnp.int32, (B, 1), 0)

    def load(p):
        band = x[rows_of(p), :].astype(jnp.float32)
        for m in range(NP):
            w = min(PR, BAND * B - m * PR)
            t32[0:B, m * PW:m * PW + w] = band[0:B, m * PR:m * PR + w]
        t32[B:PR, B:PR] = band[B:PR, 0:B]
        for m in range(1, NP):
            t32[B:PR, m * PW:m * PW + PR] = band[B:PR, m * PR - B:m * PR + B]
        half = []
        for a in range(2):
            t = jnp.clip(first + 2 * p + a, 0, tiles - 1)
            ok = jnp.where(row < B - padding[t], 1.0, 0.0)
            m = ok * mask_row(p, a)
            half.append(jnp.where(m > 0.5, t32[a * B:(a + 1) * B, :], 0.0))
        f[rows_of(p), :] = jnp.concatenate(half, axis=0).astype(jnp.bfloat16)

    def product(p, right, jj):
        total = None
        for kk in range(max(0, jj - 2), min(NP, jj + 3)):
            c = jj - kk + 2
            term = jnp.dot(f[rows_of(p), kk * PW:kk * PW + PR],
                           right[rows_of(p - 2 + kk), c * PW:(c + 1) * PW],
                           preferred_element_type=jnp.float32)
            total = term if total is None else total + term
        return total

    def both(p, jj):
        cols = slice(jj * PW, (jj + 1) * PW)
        return jnp.concatenate(
            [jnp.broadcast_to(mask_row(p, a)[:, cols], (B, PW)) for a in range(2)], axis=0)

    def square(p):
        for jj in range(NP):
            s[rows_of(p), jj * PW:(jj + 1) * PW] = (
                product(p, f, jj) * both(p, jj)).astype(jnp.bfloat16)

    def cubed(p):
        for jj in range(NP):
            cols = slice(jj * PW, (jj + 1) * PW)
            c = product(p, s, jj) * both(p, jj)
            t32[:, cols] = 3.0 * s[rows_of(p), cols].astype(jnp.float32) - 2.0 * c
        top = [t32[0:B, m * PW:m * PW + min(PR, BAND * B - m * PR)] for m in range(NP)]
        low = [t32[B:PR, B:PR]] + [t32[B:PR, m * PW:m * PW + PR] for m in range(1, NP)]
        whole = jnp.concatenate(
            [jnp.concatenate(top, axis=1), jnp.concatenate(low, axis=1)], axis=0)
        out[pl.ds(pl.multiple_of((p - FAR) * PR, 16), PR), :] = whole.astype(jnp.bfloat16)

    def at(p):
        return p + odd * (ALL - 1 - 2 * p)

    def run(body, pairs):
        lo, hi = pairs
        step = 1 if hi >= lo else -1

        def go(i, carry):
            body(at(lo + step * i))
            return carry

        lax.fori_loop(0, abs(hi - lo) + 1, go, 0)

    own.wait()
    run(load, (4, 9))
    run(square, (6, 7))

    def wait_below():
        for c in head():
            c.wait_recv()

    def wait_above():
        for c in tail():
            c.wait_recv()

    pl.when(even)(wait_below)
    pl.when(jnp.logical_not(even))(wait_above)
    run(load, (10, 13))
    run(square, (8, 11))
    run(cubed, (8, 9))

    @pl.when(even & has_up)
    def _():
        wait_above()

    @pl.when(jnp.logical_not(even) & has_down)
    def _():
        wait_below()

    @pl.when((even & has_up) | (jnp.logical_not(even) & has_down))
    def _():
        run(load, (3, 0))

    run(square, (5, 2))
    run(cubed, (7, 4))

    @pl.when(has_down)
    def _():
        for c in tail():
            c.wait_send()

    @pl.when(has_up)
    def _():
        for c in head():
            c.wait_send()


def per_device(density, tile_mask, padding):
    count = lax.axis_size("row")
    rows = density.shape[0]
    assert rows == OWN * PR
    body = functools.partial(kernel, count, tile_mask.shape[0])
    return pl.pallas_call(
        body,
        out_shape=jax.ShapeDtypeStruct(density.shape, jnp.bfloat16),
        in_specs=[
            pl.BlockSpec(memory_space=pl.ANY),
            pl.BlockSpec(memory_space=pltpu.SMEM),
            pl.BlockSpec(memory_space=pltpu.SMEM),
        ],
        out_specs=pl.BlockSpec(memory_space=pltpu.VMEM),
        scratch_shapes=[
            pltpu.VMEM((ALL * PR, BAND * B), jnp.bfloat16),
            pltpu.VMEM((ALL * PR, WIDE), jnp.bfloat16),
            pltpu.VMEM((ALL * PR, WIDE), jnp.bfloat16),
            pltpu.VMEM((PR, WIDE), jnp.float32),
            pltpu.VMEM((ALL * 16, WIDE), jnp.float32),
            pltpu.SemaphoreType.DMA((6,)),
            pltpu.SemaphoreType.DMA((6,)),
            pltpu.SemaphoreType.DMA,
        ],
        compiler_params=pltpu.CompilerParams(
            collective_id=0, has_side_effects=True, vmem_limit_bytes=52 * 1024 * 1024),
    )(density, tile_mask, padding)


def solution(mesh):
    return jax.shard_map(
        per_device,
        mesh=mesh,
        in_specs=(P(("parts", "row"), None), P("parts", None), P("parts")),
        out_specs=P(("parts", "row"), None),
        check_vma=False,
    )
```

profile of v0, /device:TPU:25, one launch (start us, length us, event | category | flops | bytes accessed | tf_op | source)
XLA Modules:
  0.0 49.7 jit_solution(223426514083343734)
XLA Ops:
  0.0 0.0 copy-start
  0.0 0.8 %copy.5.tile_mask = s32[192,9]{1,0:T(8,128)S(1)} copy(s32[192,9]{0,1:T(8,128)} %param.4) | data formatting | bytes 13824 | tf_op args[1]
  0.8 4.5 %copy.4.density = bf16[1248,936]{1,0:T(8,128)(2,1)} copy(bf16[1248,936]{0,1:T(8,128)(2,1)} %param.3) | data formatting | bytes 4672512 | tf_op args[0]
  5.3 0.0 copy-done
  5.3 40.1 %shard_map.37 = bf16[1248,936]{1,0:T(8,128)(2,1)} custom-call(bf16[1248,936]{1,0:T(8,128)(2,1)} %copy.4.density, s32[192,9]{1,0:T(8,128)S(1)} %copy.5.tile_mask, s32[192]{0:T(256)S(1)} %copy-done), custom_call_target="tpu_custom_call" | custom-call | tf_op jit(solution)/shard_map/pallas_call | solution.py:215
  45.4 4.3 %copy.6 = bf16[1248,936]{0,1:T(8,128)(2,1)} copy(bf16[1248,936]{1,0:T(8,128)(2,1)} %shard_map.37) | data formatting | bytes 4672512 | tf_op jit(solution)/shard_map/pallas_call | solution.py:215
Async XLA Ops:
  0.0 5.3 %copy-start = (s32[192]{0:T(256)S(1)}, s32[192]{0:T(256)}, u32[]{:S(2)}) copy-start(s32[192]{0:T(256)} %padding.1) | copy-start | bytes 2308
where the time goes:
time: 50 us; the launch traced here: 49.7 us
  Pallas kernels  40.1 us (80%)
  local copies, waits for them, and re-layouts  9.59 us (19%)
    pallas_call x1, Pallas kernels, per_device(): pl.pallas_call(body, out_shape=jax.ShapeDtypeStruct(density.shape, jnp.bf...  40.1 us
    unnamed x4, local copies, waits for them, and re-layouts  5.3 us
    pallas_call x1, local copies, waits for them, and re-layouts, per_device(): pl.pallas_call(body, out_shape=jax.ShapeDtypeStruct(density.shape, jnp.bf...  4.29 us

commit v1 on v0

v1 whole, which is shorter than its diff:
```python
import functools

import jax
import jax.numpy as jnp
from jax import lax
from jax.experimental import pallas as pl
from jax.experimental.pallas import tpu as pltpu
from jax.sharding import PartitionSpec as P

B = 104
H = 4
BAND = 9
PR = 2 * B
PW = 256
NP = 5
TALL = NP * PR
FULL = BAND * B
FAR = 4
OWN = 6
ALL = OWN + 2 * FAR
SKIP = (OWN * PR - FAR * PR) // 128 * 128
SIDE = 896
LAST = OWN * PR - SKIP
MESH = pl.DeviceIdType.MESH


def kernel(count, tiles, density, tile_mask, padding, out, x, up, down, f, s, t32, lv,
           send_sem, recv_sem, own_sem):
    me = lax.axis_index("row")
    odd = lax.rem(me, 2)
    even = odd == 0
    has_up = me > 0
    has_down = me < count - 1
    first = me * (2 * OWN) - 2 * FAR

    own = pltpu.make_async_copy(density, x, own_sem)
    own.start()

    barrier = pltpu.get_barrier_semaphore()

    @pl.when(has_up)
    def _():
        pl.semaphore_signal(barrier, inc=1, device_id={"row": me - 1}, device_id_type=MESH)

    @pl.when(has_down)
    def _():
        pl.semaphore_signal(barrier, inc=1, device_id={"row": me + 1}, device_id_type=MESH)

    pl.semaphore_wait(barrier, has_up.astype(jnp.int32) + has_down.astype(jnp.int32))

    def piece(row, rows, lane, width, dst, back, slot, where):
        return pltpu.make_async_remote_copy(
            src_ref=density.at[pl.ds(row, rows), pl.ds(lane, width)],
            dst_ref=dst.at[pl.ds(row, rows), pl.ds(lane - back, width)],
            send_sem=send_sem.at[slot], recv_sem=recv_sem.at[slot],
            device_id={"row": where}, device_id_type=MESH)

    def tail():
        return [piece(0, FULL, 768, 480, up, SKIP, 0, me + 1),
                piece(512, FULL - 512, 640, 128, up, SKIP, 1, me + 1),
                piece(624, FULL - 624, 512, 128, up, SKIP, 2, me + 1),
                piece(832, FULL - 832, 384, 128, up, SKIP, 3, me + 1)]

    def head():
        return [piece(0, FULL, 0, 512, down, 0, 4, me - 1),
                piece(0, 416, 512, 128, down, 0, 5, me - 1),
                piece(0, 208, 640, 128, down, 0, 6, me - 1),
                piece(0, 112, 768, 128, down, 0, 7, me - 1)]

    @pl.when(has_down)
    def _():
        for c in tail():
            c.start()

    @pl.when(has_up)
    def _():
        for c in head():
            c.start()

    lane = lax.broadcasted_iota(jnp.int32, (1, PW), 1)
    second = lane >= B

    def limits(p, carry):
        t = first + 2 * p
        tc = [jnp.clip(t + a, 0, tiles - 1) for a in range(2)]
        ok = ((lane < B - padding[tc[0]]) & (lane < B)) | (
            second & (lane < PR - padding[tc[1]]))
        for slot in range(2 * NP):
            room = B - padding[jnp.clip(t + slot - H, 0, tiles - 1)]
            top = tile_mask[slot, tc[0]] * room if slot < BAND else 0
            low = tile_mask[slot - 1, tc[1]] * room if slot else 0
            row = jnp.where(ok, jnp.where(second, low, top), 0)
            lv[pl.ds(pl.multiple_of((p * 2 * NP + slot) * 8, 8), 8), :] = (
                jnp.broadcast_to(row, (8, PW)))
        return carry

    lax.fori_loop(0, ALL, limits, 0)
    t32[...] = jnp.zeros_like(t32)
    f[...] = jnp.zeros_like(f)
    z = lax.broadcasted_iota(jnp.int32, (B, PW), 0)

    def masked(p, slot, block):
        row = lv[pl.ds(pl.multiple_of((p * 2 * NP + slot) * 8, 8), 1), :]
        return jnp.where(z < row, block, 0.0)

    def load(p):
        for q in range(ALL):
            if q < FAR:
                src, lo = up, OWN * PR - FAR * PR - SKIP + q * PR
            elif q < FAR + OWN:
                src, lo = x, (q - FAR) * PR
            else:
                src, lo = down, (q - FAR - OWN) * PR

            @pl.when(p == q)
            def _(src=src, lo=lo):
                t32[0:FULL, 0:PR] = src[:, lo:lo + PR].astype(jnp.float32)

        for m in range(NP):
            half = []
            for slot in (2 * m, 2 * m + 1):
                at_top = min(slot, BAND - 1) * B
                at_low = max(slot - 1, 0) * B
                both = jnp.where(second, t32[at_low:at_low + B, :], t32[at_top:at_top + B, :])
                half.append(masked(p, slot, both))
            f[p, m * PR:(m + 1) * PR, :] = jnp.concatenate(half, axis=0).astype(jnp.bfloat16)

    def product(p, left, jj):
        total = None
        for kk in range(max(0, jj - 2), min(NP, jj + 3)):
            c = jj - kk + 2
            term = jnp.dot(left[p - 2 + kk, c * PR:(c + 1) * PR, 0:PR],
                           f[p, kk * PR:(kk + 1) * PR, :],
                           preferred_element_type=jnp.float32)
            total = term if total is None else total + term
        return jnp.concatenate(
            [masked(p, 2 * jj + a, total[a * B:(a + 1) * B, :]) for a in range(2)], axis=0)

    def square(p):
        for jj in range(NP):
            s[p, jj * PR:(jj + 1) * PR, :] = product(p, f, jj).astype(jnp.bfloat16)

    def cubed(p):
        for jj in range(NP):
            rows = slice(jj * PR, (jj + 1) * PR)
            t32[rows, :] = 3.0 * s[p, rows, :].astype(jnp.float32) - 2.0 * product(p, s, jj)
        whole = jnp.where(second, t32[B:TALL, :], t32[0:FULL, :]).astype(jnp.bfloat16)
        for q in range(OWN):
            @pl.when(p == q + FAR)
            def _(q=q):
                out[:, q * PR:(q + 1) * PR] = whole[:, 0:PR]

    def at(p):
        return p + odd * (ALL - 1 - 2 * p)

    def run(body, pairs):
        lo, hi = pairs
        step = 1 if hi >= lo else -1

        def go(i, carry):
            body(at(lo + step * i))
            return carry

        lax.fori_loop(0, abs(hi - lo) + 1, go, 0)

    own.wait()
    run(load, (4, 9))
    run(square, (6, 7))

    def wait_below():
        for c in head():
            c.wait_recv()

    def wait_above():
        for c in tail():
            c.wait_recv()

    pl.when(even)(wait_below)
    pl.when(jnp.logical_not(even))(wait_above)
    run(load, (10, 13))
    run(square, (8, 11))
    run(cubed, (8, 9))

    @pl.when(even & has_up)
    def _():
        wait_above()

    @pl.when(jnp.logical_not(even) & has_down)
    def _():
        wait_below()

    @pl.when((even & has_up) | (jnp.logical_not(even) & has_down))
    def _():
        run(load, (3, 0))

    run(square, (5, 2))
    run(cubed, (7, 4))

    @pl.when(has_down)
    def _():
        for c in tail():
            c.wait_send()

    @pl.when(has_up)
    def _():
        for c in head():
            c.wait_send()


def per_device(density, tile_mask, padding):
    count = lax.axis_size("row")
    rows = density.shape[0]
    assert rows == OWN * PR
    body = functools.partial(kernel, count, tile_mask.shape[0])
    return pl.pallas_call(
        body,
        out_shape=jax.ShapeDtypeStruct((FULL, rows), jnp.bfloat16),
        in_specs=[
            pl.BlockSpec(memory_space=pl.ANY),
            pl.BlockSpec(memory_space=pltpu.SMEM),
            pl.BlockSpec(memory_space=pltpu.SMEM),
        ],
        out_specs=pl.BlockSpec(memory_space=pltpu.VMEM),
        scratch_shapes=[
            pltpu.VMEM((FULL, OWN * PR), jnp.bfloat16),
            pltpu.VMEM((FULL, LAST), jnp.bfloat16),
            pltpu.VMEM((FULL, SIDE), jnp.bfloat16),
            pltpu.VMEM((ALL, TALL, PW), jnp.bfloat16),
            pltpu.VMEM((ALL, TALL, PW), jnp.bfloat16),
            pltpu.VMEM((TALL, PW), jnp.float32),
            pltpu.VMEM((ALL * 2 * NP * 8, PW), jnp.int32),
            pltpu.SemaphoreType.DMA((8,)),
            pltpu.SemaphoreType.DMA((8,)),
            pltpu.SemaphoreType.DMA,
        ],
        compiler_params=pltpu.CompilerParams(
            collective_id=0, has_side_effects=True, vmem_limit_bytes=52 * 1024 * 1024),
    )(density.T, tile_mask.T, padding).T


def solution(mesh):
    return jax.shard_map(
        per_device,
        mesh=mesh,
        in_specs=(P(("parts", "row"), None), P("parts", None), P("parts")),
        out_specs=P(("parts", "row"), None),
        check_vma=False,
    )
```

time: 50 us -> 43.7 us (0.87)
  local copies, waits for them, and re-layouts: 9.59 us -> 4.64 us
  Pallas kernels: 40.1 us -> 38.7 us
    pallas_call x1 -> x0, local copies, waits for them, and re-layouts: 4.29 us -> none  [per_device(): pl.pallas_call(body, out_shape=jax.ShapeDtypeStruct(density.shape, jnp.bf...]
    pallas_call x1, Pallas kernels: 40.1 us -> 38.7 us  [per_device(): pl.pallas_call(body, out_shape=jax.ShapeDtypeStruct((FULL, rows), jnp.bfl...]
    unnamed x4 -> x5, local copies, waits for them, and re-layouts: 5.3 us -> 4.64 us
where the time goes in v1:
time: 43.7 us; the launch traced here: 43.4 us
  Pallas kernels  38.7 us (89%)
  local copies, waits for them, and re-layouts  4.64 us (11%)
    pallas_call x1, Pallas kernels, per_device(): pl.pallas_call(body, out_shape=jax.ShapeDtypeStruct((FULL, rows), jnp.bfl...  38.7 us
    unnamed x5, local copies, waits for them, and re-layouts  4.64 us

profile of v1, /device:TPU:25, one launch (start us, length us, event | category | flops | bytes accessed | tf_op | source)
XLA Modules:
  0.0 43.4 jit_solution(6240573128098245002)
XLA Ops:
  0.0 0.0 copy-start
  0.0 0.7 %copy-done = s32[192,9]{0,1:T(8,128)S(1)} copy-done((s32[192,9]{0,1:T(8,128)S(1)}, s32[192,9]{0,1:T(8,128)}, u32[]{:S(2)}) %copy-start) | copy-done | bytes 6936
  0.7 0.0 copy-start.1
  0.7 0.7 %copy-done.1 = s32[192]{0:T(256)S(1)} copy-done((s32[192]{0:T(256)S(1)}, s32[192]{0:T(256)}, u32[]{:S(2)}) %copy-start.1) | copy-done | bytes 792
  1.4 38.7 %shard_map.37 = bf16[936,1248]{1,0:T(8,128)(2,1)} custom-call(bf16[936,1248]{1,0:T(8,128)(2,1)} %bitcast.5, s32[9,192]{1,0:T(8,128)S(1)} %bitcast.3, s32[192]{0:T(256)S(1)} %copy-done.1), custom_call_target="tpu_custom_call" | custom-call | tf_op jit(solution)/shard_map/pallas_call | solution.py:215
  40.1 3.2 %copy.5 = bf16[1248,936]{0,1:T(8,128)(2,1)} copy(bf16[1248,936]{0,1:T(8,128)(2,1)} %bitcast.4) | data formatting | bytes 4672512
Async XLA Ops:
  0.0 0.7 %copy-start = (s32[192,9]{0,1:T(8,128)S(1)}, s32[192,9]{0,1:T(8,128)}, u32[]{:S(2)}) copy-start(s32[192,9]{0,1:T(8,128)} %param.4) | copy-start | bytes 20740
  0.7 0.7 %copy-start.1 = (s32[192]{0:T(256)S(1)}, s32[192]{0:T(256)}, u32[]{:S(2)}) copy-start(s32[192]{0:T(256)} %padding.1) | copy-start | bytes 2308

commit v2 on v1

--- a/solution.py
+++ b/solution.py
@@ -56,25 +56,30 @@
             device_id={"row": where}, device_id_type=MESH)
 
     def tail():
-        return [piece(0, FULL, 768, 480, up, SKIP, 0, me + 1),
-                piece(512, FULL - 512, 640, 128, up, SKIP, 1, me + 1),
-                piece(624, FULL - 624, 512, 128, up, SKIP, 2, me + 1),
-                piece(832, FULL - 832, 384, 128, up, SKIP, 3, me + 1)]
+        return [[piece(0, FULL, 1024, 224, up, SKIP, 0, me + 1)],
+                [piece(0, FULL, 768, 256, up, SKIP, 1, me + 1)],
+                [piece(512, FULL - 512, 640, 128, up, SKIP, 2, me + 1),
+                 piece(624, FULL - 624, 512, 128, up, SKIP, 3, me + 1)],
+                [piece(832, FULL - 832, 384, 128, up, SKIP, 4, me + 1)]]
 
     def head():
-        return [piece(0, FULL, 0, 512, down, 0, 4, me - 1),
-                piece(0, 416, 512, 128, down, 0, 5, me - 1),
-                piece(0, 208, 640, 128, down, 0, 6, me - 1),
-                piece(0, 112, 768, 128, down, 0, 7, me - 1)]
+        return [[piece(0, FULL, 0, 256, down, 0, 5, me - 1)],
+                [piece(0, FULL, 256, 256, down, 0, 6, me - 1)],
+                [piece(0, 416, 512, 128, down, 0, 7, me - 1),
+                 piece(0, 208, 640, 128, down, 0, 8, me - 1)],
+                [piece(0, 112, 768, 128, down, 0, 9, me - 1)]]
+
+    def each(stages):
+        return [c for stage in stages for c in stage]
 
     @pl.when(has_down)
     def _():
-        for c in tail():
+        for c in each(tail()):
             c.start()
 
     @pl.when(has_up)
     def _():
-        for c in head():
+        for c in each(head()):
             c.start()
 
     lane = lax.broadcasted_iota(jnp.int32, (1, PW), 1)
@@ -168,11 +173,11 @@
     run(square, (6, 7))
 
     def wait_below():
-        for c in head():
+        for c in each(head()):
             c.wait_recv()
 
     def wait_above():
-        for c in tail():
+        for c in each(tail()):
             c.wait_recv()
 
     pl.when(even)(wait_below)
@@ -181,29 +186,39 @@
     run(square, (8, 11))
     run(cubed, (8, 9))
 
-    @pl.when(even & has_up)
-    def _():
-        wait_above()
-
-    @pl.when(jnp.logical_not(even) & has_down)
-    def _():
-        wait_below()
-
-    @pl.when((even & has_up) | (jnp.logical_not(even) & has_down))
-    def _():
-        run(load, (3, 0))
-
-    run(square, (5, 2))
-    run(cubed, (7, 4))
+    from_above = even & has_up
+    from_below = jnp.logical_not(even) & has_down
+
+    def stage(i, carry):
+        for k in range(FAR):
+            @pl.when(from_above & (i == k))
+            def _(k=k):
+                for c in tail()[k]:
+                    c.wait_recv()
+
+            @pl.when(from_below & (i == k))
+            def _(k=k):
+                for c in head()[k]:
+                    c.wait_recv()
+
+        @pl.when(from_above | from_below)
+        def _():
+            load(at(FAR - 1 - i))
+
+        square(at(FAR + 1 - i))
+        cubed(at(FAR + 3 - i))
+        return carry
+
+    lax.fori_loop(0, FAR, stage, 0)
 
     @pl.when(has_down)
     def _():
-        for c in tail():
+        for c in each(tail()):
             c.wait_send()
 
     @pl.when(has_up)
     def _():
-        for c in head():
+        for c in each(head()):
             c.wait_send()
 
 
@@ -229,8 +244,8 @@
             pltpu.VMEM((ALL, TALL, PW), jnp.bfloat16),
             pltpu.VMEM((TALL, PW), jnp.float32),
             pltpu.VMEM((ALL * 2 * NP * 8, PW), jnp.int32),
-            pltpu.SemaphoreType.DMA((8,)),
-            pltpu.SemaphoreType.DMA((8,)),
+            pltpu.SemaphoreType.DMA((10,)),
+            pltpu.SemaphoreType.DMA((10,)),
             pltpu.SemaphoreType.DMA,
         ],
         compiler_params=pltpu.CompilerParams(

time: 43.7 us -> 40.1 us (0.918)
  Pallas kernels: 38.7 us -> 35.2 us
    pallas_call x1, Pallas kernels: 38.7 us -> 35.2 us  [per_device(): pl.pallas_call(body, out_shape=jax.ShapeDtypeStruct((FULL, rows), jnp.bfl...]
where the time goes in v2:
time: 40.1 us; the launch traced here: 39.8 us
  Pallas kernels  35.2 us (88%)
  local copies, waits for them, and re-layouts  4.64 us (12%)
    pallas_call x1, Pallas kernels, per_device(): pl.pallas_call(body, out_shape=jax.ShapeDtypeStruct((FULL, rows), jnp.bfl...  35.2 us
    unnamed x5, local copies, waits for them, and re-layouts  4.64 us

profile of v2, /device:TPU:25, one launch (start us, length us, event | category | flops | bytes accessed | tf_op | source)
XLA Modules:
  0.0 39.8 jit_solution(7293920584405151615)
XLA Ops:
  0.0 0.0 copy-start
  0.0 0.7 %copy-done = s32[192,9]{0,1:T(8,128)S(1)} copy-done((s32[192,9]{0,1:T(8,128)S(1)}, s32[192,9]{0,1:T(8,128)}, u32[]{:S(2)}) %copy-start) | copy-done | bytes 6936
  0.7 0.0 copy-start.1
  0.7 0.7 %copy-done.1 = s32[192]{0:T(256)S(1)} copy-done((s32[192]{0:T(256)S(1)}, s32[192]{0:T(256)}, u32[]{:S(2)}) %copy-start.1) | copy-done | bytes 792
  1.4 35.2 %shard_map.37 = bf16[936,1248]{1,0:T(8,128)(2,1)} custom-call(bf16[936,1248]{1,0:T(8,128)(2,1)} %bitcast.5, s32[9,192]{1,0:T(8,128)S(1)} %bitcast.3, s32[192]{0:T(256)S(1)} %copy-done.1), custom_call_target="tpu_custom_call" | custom-call | tf_op jit(solution)/shard_map/pallas_call | solution.py:230
  36.6 3.2 %copy.5 = bf16[1248,936]{0,1:T(8,128)(2,1)} copy(bf16[1248,936]{0,1:T(8,128)(2,1)} %bitcast.4) | data formatting | bytes 4672512
Async XLA Ops:
  0.0 0.7 %copy-start = (s32[192,9]{0,1:T(8,128)S(1)}, s32[192,9]{0,1:T(8,128)}, u32[]{:S(2)}) copy-start(s32[192,9]{0,1:T(8,128)} %param.4) | copy-start | bytes 20740
  0.7 0.7 %copy-start.1 = (s32[192]{0:T(256)S(1)}, s32[192]{0:T(256)}, u32[]{:S(2)}) copy-start(s32[192]{0:T(256)} %padding.1) | copy-start | bytes 2308
